TPU v7x, 256 devices: a whole 4x4x8 slice. The times are simulated.
256 devices in a mesh: ctx: 16 (over x, y_hi, core), head: 16 (over z, y_lo).
Axes of the slice: x: 4, y: 4 (y_hi: 2, y_lo: 2; y = y_hi * 2 + y_lo), z: 8, core: 2. Of those that a mesh axis runs over, the one named last changes fastest.
Arguments:
- latent: bfloat16 [2048, 576], P('ctx'), may hold values from -6 to 6
- query: bfloat16 [2048, 12288], P('ctx', 'head'), may hold values from -20 to 20
- up_key: bfloat16 [512, 8192], P(None, 'head'), may hold values from -0.25 to 0.25
- up_value: bfloat16 [512, 8192], P(None, 'head'), may hold values from -1 to 1
- out_grad: bfloat16 [2048, 8192], P('ctx', 'head'), may hold values from -6 to 6
- block_pos: int32 [32], replicated, may hold values from 0 to 31, each once
Outputs:
- attention_out: bfloat16 [2048, 8192], P('ctx', 'head')
- query_grad: bfloat16 [2048, 12288], P('ctx', 'head')
- latent_grad: float32 [2048, 576], P(('ctx', 'head'))
- up_key_grad: float32 [512, 8192], P('ctx', 'head')
- up_value_grad: float32 [512, 8192], P('ctx', 'head')
Inputs may be any that keep to these rules, and one draw needn't show every extreme that they name: `block_pos`: every half-block position appears exactly once.
All inputs are finite; a program needn't handle non-finite values.
Results may differ from a plain program's by a relative error of at most 0.035.
Values may be sent and summed in bfloat16 or wider, within the bound.
A program may use at most 64 MiB of HBM per device.

v0:
```python
import math

import jax
import jax.numpy as jnp
from jax import lax
from jax.sharding import PartitionSpec as P

LATENT = 512
ROPE = 64
NOPE = 128
VDIM = 128


start_max = -1e30


def token_positions(row_ids, block_pos, half_rows):
    blocks = row_ids // half_rows
    onehot = blocks[:, None] == jnp.arange(block_pos.shape[0], dtype=jnp.int32)[None, :]
    first = jnp.sum(jnp.where(onehot, block_pos[None, :], 0), axis=1)
    return first * half_rows + row_ids % half_rows


def on_device(latent, query, up_key, up_value, out_grad, block_pos):
    rows_dev = latent.shape[0]
    half_rows = rows_dev // 2
    heads_dev = up_key.shape[1] // NOPE
    qk_width = NOPE + ROPE
    score_scale = 1.0 / math.sqrt(qk_width)
    seq_rows = rows_dev * lax.axis_size("ctx")
    own_start = lax.axis_index("ctx") * rows_dev
    query_pos = token_positions(
        own_start + jnp.arange(rows_dev, dtype=jnp.int32), block_pos, half_rows
    )
    queries = query.reshape(rows_dev, heads_dev, qk_width)
    grads_out = out_grad.reshape(rows_dev, heads_dev, VDIM)
    w_both = jnp.concatenate([up_key, up_value], 1)

    def project(nope_rows):
        return jnp.dot(nope_rows, w_both, preferred_element_type=jnp.float32).astype(jnp.bfloat16)

    def split_kv(key_values, rope_rows):
        piece_rows = key_values.shape[0]
        key_nope = key_values[:, : heads_dev * NOPE].reshape(piece_rows, heads_dev, NOPE)
        values = key_values[:, heads_dev * NOPE :].reshape(piece_rows, heads_dev, VDIM)
        rope_wide = jnp.broadcast_to(rope_rows[:, None, :], (piece_rows, heads_dev, ROPE))
        return (jnp.concatenate([key_nope, rope_wide], 2), values)

    def unpack(pieces):
        return split_kv(project(pieces[:, :LATENT]), pieces[:, LATENT:])

    def visibility(piece_rows):
        key_pos = token_positions(jnp.arange(piece_rows, dtype=jnp.int32), block_pos, half_rows)
        return query_pos[:, None] >= key_pos[None, :]

    def scores(key_rows, visible):
        logits = (
            jnp.einsum("qhd,khd->hqk", queries, key_rows, preferred_element_type=jnp.float32)
            * score_scale
        )
        return jnp.where(visible[None], logits, jnp.float32(-jnp.inf))

    initial = (
        jnp.full((heads_dev, rows_dev), start_max, jnp.float32),
        jnp.zeros((heads_dev, rows_dev), jnp.float32),
        jnp.zeros((heads_dev, rows_dev, VDIM), jnp.float32),
    )
    key_rows, values = unpack(lax.all_gather(latent, "ctx", axis=0, tiled=True))
    visible = visibility(key_rows.shape[0])

    def update(state):
        run_max, run_sum, run_out = state
        logits = scores(key_rows, visible)
        new_max = jnp.maximum(run_max, jnp.max(logits, axis=2))
        weights = jnp.exp(logits - new_max[:, :, None])
        new_sum = jnp.sum(weights, axis=2)
        added = jnp.einsum(
            "hqk,khd->hqd", weights.astype(jnp.bfloat16), values, preferred_element_type=jnp.float32
        )
        return (new_max, new_sum, added)

    run_max, run_sum, run_out = update(initial)
    output_low = (run_out / run_sum[:, :, None]).astype(jnp.bfloat16)
    output_rows = output_low.transpose(1, 0, 2)
    attention_out = output_rows.reshape(rows_dev, heads_dev * VDIM)
    log_total = run_max + jnp.log(run_sum)
    row_delta = jnp.sum(grads_out.astype(jnp.float32) * output_rows.astype(jnp.float32), axis=2).T

    def gradients(key_rows, values, visible):
        piece_rows = key_rows.shape[0]
        prob = jnp.exp(scores(key_rows, visible) - log_total[:, :, None])
        prob_low = prob.astype(jnp.bfloat16)
        value_grad = jnp.einsum(
            "hqk,qhd->khd", prob_low, grads_out, preferred_element_type=jnp.float32
        )
        prob_grad = jnp.einsum(
            "qhd,khd->hqk", grads_out, values, preferred_element_type=jnp.float32
        )
        score_grad = (prob * (prob_grad - row_delta[:, :, None])).astype(jnp.bfloat16)
        query_add = jnp.einsum(
            "hqk,khd->qhd", score_grad, key_rows, preferred_element_type=jnp.float32
        )
        key_grad = (
            jnp.einsum("hqk,qhd->khd", score_grad, queries, preferred_element_type=jnp.float32)
            * score_scale
        )
        key_nope_grad = key_grad[:, :, :NOPE].reshape(piece_rows, heads_dev * NOPE)
        rope_grad = jnp.sum(key_grad[:, :, NOPE:], axis=1)
        return (
            query_add,
            key_nope_grad,
            value_grad.reshape(piece_rows, heads_dev * VDIM),
            rope_grad,
        )

    key_weight_t = up_key.T
    value_weight_t = up_value.T
    start_back = (
        jnp.zeros((rows_dev, heads_dev, qk_width), jnp.float32),
        jnp.zeros((seq_rows, LATENT + ROPE), jnp.float32),
        jnp.zeros((LATENT, heads_dev * NOPE), jnp.float32),
        jnp.zeros((LATENT, heads_dev * VDIM), jnp.float32),
    )
    pieces = lax.all_gather(latent, "ctx", axis=0, tiled=True)
    fold_key_rows, fold_values = unpack(pieces)
    piece_rows = fold_key_rows.shape[0]
    fold_visible = visibility(piece_rows)

    def update(state):
        query_add, key_nope_grad, value_grad, rope_grad = gradients(
            fold_key_rows, fold_values, fold_visible
        )
        key_low = key_nope_grad.astype(jnp.bfloat16)
        value_low = value_grad.astype(jnp.bfloat16)
        nope_grad = jnp.dot(key_low, key_weight_t, preferred_element_type=jnp.float32)
        nope_grad = nope_grad + jnp.dot(
            value_low, value_weight_t, preferred_element_type=jnp.float32
        )
        current = jnp.concatenate([nope_grad, rope_grad], 1)
        nope_rows_t = pieces[:, :LATENT].T
        key_wgrad = jnp.dot(nope_rows_t, key_low, preferred_element_type=jnp.float32)
        value_wgrad = jnp.dot(nope_rows_t, value_low, preferred_element_type=jnp.float32)
        return (query_add, current, key_wgrad, value_wgrad)

    query_acc, lat_acc, key_wgrad, value_wgrad = update(start_back)
    latent_grad = lax.psum_scatter(lat_acc, ("ctx", "head"), scatter_dimension=0, tiled=True)
    up_key_grad, up_value_grad = (
        lax.psum_scatter(key_wgrad, "ctx", scatter_dimension=0, tiled=True),
        lax.psum_scatter(value_wgrad, "ctx", scatter_dimension=0, tiled=True),
    )
    query_grad = (
        (query_acc * score_scale).astype(jnp.bfloat16).reshape(rows_dev, heads_dev * qk_width)
    )
    return (attention_out, query_grad, latent_grad, up_key_grad, up_value_grad)


def solution(mesh):
    in_specs = (
        P("ctx", None),
        P("ctx", "head"),
        P(None, "head"),
        P(None, "head"),
        P("ctx", "head"),
        P(),
    )
    out_specs = (
        P("ctx", "head"),
        P("ctx", "head"),
        P(("ctx", "head"), None),
        P("ctx", "head"),
        P("ctx", "head"),
    )
    return jax.shard_map(
        on_device, mesh=mesh, in_specs=in_specs, out_specs=out_specs, check_vma=False
    )
```

profile of v0, /device:TPU:2, one launch (start us, length us, event | category | flops | bytes accessed | tf_op | source)
XLA Modules:
  0.0 520.7 jit_solution(2193592370460375417)
XLA Ops:
  7.2 0.0 all-gather.2.cloned.1.call-start
  7.2 0.7 all-gather.2.cloned.1.call-update
  7.9 0.0 all-reduce.3.cloned.1.call-start
  7.9 1.0 copy.53
  9.0 1.1 copy.51
  10.1 0.7 select_reduce_fusion.1
  10.8 0.8 select_reduce_fusion
  11.6 0.3 broadcast_compare_fusion
  12.0 57.0 %all-gather.2.cloned.1.call-done = bf16[2048,576]{0,1:T(8,128)(2,1)} async-done(((bf16[128,576]{0,1:T(8,128)(2,1)}), bf16[2048,576]{0,1:T(8,128)(2,1)}) %all-gather.2.cloned.1.call-update) | async-done | bytes 2359312 | tf_op jit(solution)/shard_map/all_gather | solution.py:68
  69.0 4.3 convert_bitcast_fusion
  73.3 0.0 slice-start
  73.3 0.6 fusion.47
  73.9 0.0 copy-start.3
  73.9 0.3 slice-done
  74.2 0.1 broadcast_in_dim.81
  74.4 2.0 fusion.48
  76.4 0.0 copy-done.3
  76.4 0.6 fusion.1
  77.0 1.1 multiply_reduce_fusion
  78.0 0.8 convolution_convert_fusion
  78.8 0.0 copy-start.2
  78.8 1.4 fusion
  80.2 0.0 copy-start
  80.2 1.0 multiply_bitcast_fusion
  81.2 0.3 copy-done
  81.5 0.0 copy-start.5
  81.5 0.1 slice_reduce_fusion
  81.6 0.3 slice.48
  81.9 0.6 copy-done.5
  82.5 0.0 copy-start.4
  82.6 1.3 fusion.49
  83.9 0.0 copy-done.2
  83.9 0.0 copy-done.4
  83.9 1.3 convolution_add_fusion
  85.1 2.5 pad_maximum_fusion
  87.6 0.0 all-reduce.3.cloned.1.call-update
  87.6 0.2 reduce-scatter.10.cloned.1.call-start
  87.9 4.5 fusion.18
  92.4 2.5 copy.74
  94.9 0.0 reduce-scatter.10.cloned.1.call-update
  94.9 0.0 reduce-scatter.8.cloned.1.call-start
  95.0 3.9 fusion.15
  98.8 0.0 copy-start.1
  98.8 2.7 copy.72
  101.5 0.0 reduce-scatter.8.cloned.1.call-update
  101.6 0.0 copy-done.1
  101.6 2.6 fusion.22
  104.1 0.8 copy.60
  105.0 0.8 copy.59
  105.7 252.2 %all-reduce.3.cloned.1.call-done = f32[2048,576]{0,1:T(8,128)} async-done(((f32[2048,576]{0,1:T(8,128)}), f32[2048,576]{0,1:T(8,128)}) %all-reduce.3.cloned.1.call-update) | async-done | bytes 4718608
  357.9 1.1 constant_dynamic-slice_fusion
  359.0 0.7 copy.61
  359.8 76.2 %reduce-scatter.10.cloned.1.call-done = f32[32,512]{1,0:T(8,128)} async-done(((f32[512,512]{1,0:T(8,128)}), f32[32,512]{1,0:T(8,128)}) %reduce-scatter.10.cloned.1.call-update) | async-done | bytes 65552
  436.0 78.2 %reduce-scatter.8.cloned.1.call-done = f32[32,512]{1,0:T(8,128)} async-done(((f32[512,512]{1,0:T(8,128)}), f32[32,512]{1,0:T(8,128)}) %reduce-scatter.8.cloned.1.call-update) | async-done | bytes 65552
  (6 shorter events, 0.0 us)
Async XLA Ops:
  7.2 61.8 %all-gather.2.cloned.1.call-start = ((), (), s32[]{:S(2)}) async-start(), calls=%async_computation.2 | async-start | bytes 2506752 | tf_op jit(solution)/shard_map/all_gather | solution.py:68
  7.9 350.0 %all-reduce.3.cloned.1.call-start = ((), (), s32[]{:S(2)}) async-start(), calls=%async_computation.5 | async-start | bytes 9437184
  73.3 1.0 slice-start
  73.9 2.5 copy-start.3
  78.8 5.0 copy-start.2
  80.2 1.3 copy-start
  81.5 1.0 copy-start.5
  82.5 1.3 copy-start.4
  87.6 348.4 %reduce-scatter.10.cloned.1.call-start = ((), (), s32[]{:S(2)}) async-start(), calls=%async_computation.4 | async-start | bytes 1114112
  94.9 419.2 %reduce-scatter.8.cloned.1.call-start = ((), (), s32[]{:S(2)}) async-start(), calls=%async_computation.3 | async-start | bytes 1114112
  98.8 2.7 copy-start.1
Sparse Core Ops, SparseCore 0:
  10.5 58.3 all-gather.1
  87.8 270.0 all-reduce.2
  363.2 72.7 reduce-scatter.9
  440.5 73.5 reduce-scatter.7
where the time goes:
time: 521 us
  waiting for transfers between devices  464 us (89%)
  matrix products  24 us (5%)
  between operations  14 us (3%)
  local copies, waits for them, and re-layouts  13.1 us (3%)
    unnamed x7, waiting for transfers between devices  407 us
    all_gather x1, waiting for transfers between devices, on_device(): key_rows, values = unpack(lax.all_gather(latent, 'ctx', axis=0, tiled=True))  57 us
    unnamed x20, local copies, waits for them, and re-layouts  11.7 us
  transfers between devices with their start and end apart: 4, of which 4 were waited for; matrix products, arithmetic and copies ran while one was open for 5% of the time, Pallas kernels for 0%

commit v1 on v0

v1 whole, which is shorter than its diff:
```python
import functools
import math

import jax
import jax.numpy as jnp
from jax import lax
from jax.experimental import pallas as pl
from jax.experimental.pallas import tpu as pltpu
from jax.sharding import PartitionSpec as P

LATENT = 512
ROPE = 64
WIDTH = LATENT + ROPE
NOPE = 128
VDIM = 128
QK = NOPE + ROPE
ROWS = 128
HEADS_DEV = 4
STACK = HEADS_DEV * ROWS
SEQ = 2048
SCALE = 1.0 / math.sqrt(QK)
LOG2E = 1.4426950408889634
MASKED = -1e30

BF = jnp.bfloat16
F32 = jnp.float32


def dot(a, b):
    return jnp.dot(a, b, preferred_element_type=F32)


def flip(a):
    return a.astype(F32).T


def slot(i, dk, dy):
    return i * 4 + dk * 2 + dy


def other(a, flip_it):
    return 1 - a if flip_it else a


def kernel(
    latent_t_hbm, query_hbm, wk_hbm, wv_hbm, dout_hbm, bpos,
    out_ref, dq_ref, dlat_ref, dwk_ref, dwv_ref,
    lat, lat_t, q_v, wk, wv, do_v, wk_t, wv_t, q_t, do_t, q_nope,
    qs_t, qd, q_rope, dlift, dos_t, scores, ed, lift_acc, lift_t, o_t, dq_t, dql,
    top, delta_row, part, r_sib, x_first, r_x1, a_1, r_y1, y_first, r_y2, a_2, r_x2,
    to_z, r_z, w_own, w_sib, w_acc, w_r,
    load_sem, send_sem, recv_sem,
):
    ctx, head = lax.axis_index("ctx"), lax.axis_index("head")
    x, yh, core = lax.div(ctx, 4), lax.rem(lax.div(ctx, 2), 2), lax.rem(ctx, 2)
    z, yl = lax.div(head, 2), lax.rem(head, 2)

    def x_at(i):
        return lax.rem(x + i, 4)

    def dev(i, dy, dk, dz, dl):
        xx, yy, kk = x_at(i), other(yh, dy), other(core, dk)
        return ((xx * 2 + yy) * 2 + kk, lax.rem(z + dz, 8) * 2 + other(yl, dl))

    sib = dev(0, 0, 1, 0, 0)
    near_y = dev(0, 1, 0, 0, 1)
    along_x = [None] + [dev(i, 0, 0, 0, 0) for i in range(1, 4)]
    y_steps = [(0, 1), (1, 0), (1, 1)]
    along_y = [dev(0, dy, 0, 0, dl) for dy, dl in y_steps]
    along_z = [dev(0, 0, 0, d, 0) for d in range(1, 8)]
    plane_steps = [(i, dy) for i in range(4) for dy in range(2)][1:]
    plane = [dev(i, dy, 0, 0, 0) for i, dy in plane_steps]

    loads = [
        pltpu.make_async_copy(src, dst, load_sem.at[n])
        for n, (src, dst) in enumerate(
            [
                (latent_t_hbm, lat_t.at[0]),
                (query_hbm, q_v),
                (wk_hbm, wk),
                (dout_hbm, do_v),
                (wv_hbm, wv),
            ]
        )
    ]
    for load in loads:
        load.start()

    barrier = pltpu.get_barrier_semaphore()
    partners = [sib] + plane + [along_y[0], along_y[2]] + along_z
    for partner in partners:
        pl.semaphore_signal(barrier, inc=1, device_id=partner, device_id_type=pl.DeviceIdType.MESH)
    pl.semaphore_wait(barrier, len(partners))

    started = []

    def send(src, dst, to):
        n = len(started)
        copy = pltpu.make_async_remote_copy(
            src_ref=src, dst_ref=dst, send_sem=send_sem.at[n], recv_sem=recv_sem.at[n],
            device_id=to, device_id_type=pl.DeviceIdType.MESH,
        )
        copy.start()
        started.append(copy)
        return copy

    def block(i, dk, dy):
        return lat_t.at[slot(i, dk, dy)]

    def pass_on(i, dy):
        return send(block(i, 0, dy), block(i, 1, dy), sib)

    loads[0].wait()
    own = lat_t.at[0]
    from_x2 = send(own, block(2, 0, 0), along_x[2])
    from_y = send(own, block(0, 0, 1), near_y)
    from_x3 = send(own, block(3, 0, 0), along_x[1])
    from_x1 = send(own, block(1, 0, 0), along_x[3])
    sib_got = {(0, 0): pass_on(0, 0)}

    for load in loads[1:]:
        load.wait()

    def lift_queries():
        q_t[...] = flip(q_v[...]).astype(BF)
        do_t[...] = flip(do_v[...]).astype(BF)
        for h in range(HEADS_DEV):
            cols = slice(h * ROWS, (h + 1) * ROWS)
            q_h_t = q_t[h * QK : h * QK + NOPE, :]
            q_lift = dot(wk[:, cols], q_h_t)
            qs_t[:LATENT, cols] = (q_lift * (SCALE * LOG2E)).astype(BF)
            rope_t = q_t[h * QK + NOPE : (h + 1) * QK, :].astype(F32)
            qs_t[LATENT:, cols] = (rope_t * (SCALE * LOG2E)).astype(BF)

    lift_queries()
    query_row = lax.broadcasted_iota(jnp.int32, (1, STACK), 1)
    query_pos = (
        jnp.where(lax.rem(query_row, 128) < 64, bpos[2 * ctx], bpos[2 * ctx + 1]) * 64
        + lax.rem(query_row, 64)
    )
    top[...] = jnp.full(top.shape, MASKED, F32)
    key_row = lax.broadcasted_iota(jnp.int32, (ROWS, 1), 0)

    def score_block(i, dk, dy):
        rows = pl.ds(slot(i, dk, dy) * ROWS, ROWS)
        owner = (x_at(i) * 2 + other(yh, dy)) * 2 + other(core, dk)
        keys = flip(lat_t[slot(i, dk, dy)]).astype(BF)
        lat[rows, :] = keys
        key_pos = (
            jnp.where(key_row < 64, bpos[2 * owner], bpos[2 * owner + 1]) * 64
            + lax.rem(key_row, 64)
        )
        s = jnp.where(key_pos <= query_pos, dot(keys, qs_t[...]), MASKED)
        scores[rows, :] = s
        top[...] = jnp.maximum(top[...], jnp.max(s.reshape(ROWS // 8, 8, STACK), axis=0))

    score_block(0, 0, 0)
    from_y.wait_recv()
    up_x3 = send(block(0, 0, 1), block(3, 0, 1), along_x[1])
    up_x1 = send(block(0, 0, 1), block(1, 0, 1), along_x[3])
    sib_got[0, 1] = pass_on(0, 1)
    sib_got[0, 0].wait_recv()
    score_block(0, 1, 0)
    from_x2.wait_recv()
    up_y = send(block(2, 0, 0), block(2, 0, 1), near_y)
    sib_got[2, 0] = pass_on(2, 0)
    from_x3.wait_recv()
    sib_got[3, 0] = pass_on(3, 0)
    from_x1.wait_recv()
    sib_got[1, 0] = pass_on(1, 0)
    score_block(0, 0, 1)
    score_block(2, 0, 0)
    score_block(3, 0, 0)
    score_block(1, 0, 0)

    def lift_rest():
        wk_t[...] = flip(wk[...]).astype(BF)
        wv_t[...] = flip(wv[...]).astype(BF)
        for h in range(HEADS_DEV):
            cols = slice(h * ROWS, (h + 1) * ROWS)
            q_nope[:, cols] = flip(q_t[h * QK : h * QK + NOPE, :]).astype(BF)
            rope = flip(q_t[h * QK + NOPE : (h + 1) * QK, :])
            q_rope[cols, :] = (rope * SCALE).astype(BF)
            qd[cols, :] = (dot(q_nope[:, cols], wk_t[cols, :]) * SCALE).astype(BF)
            dlift[:, cols] = dot(wv[:, cols], do_t[cols, :])

    lift_rest()
    sib_got[0, 1].wait_recv()
    score_block(0, 1, 1)
    sib_got[2, 0].wait_recv()
    score_block(2, 1, 0)
    up_x3.wait_recv()
    sib_got[3, 1] = pass_on(3, 1)
    up_x1.wait_recv()
    sib_got[1, 1] = pass_on(1, 1)
    sib_got[3, 0].wait_recv()
    score_block(3, 1, 0)
    sib_got[1, 0].wait_recv()
    score_block(1, 1, 0)
    up_y.wait_recv()
    sib_got[2, 1] = pass_on(2, 1)
    score_block(3, 0, 1)
    score_block(1, 0, 1)
    score_block(2, 0, 1)
    sib_got[3, 1].wait_recv()
    score_block(3, 1, 1)
    sib_got[1, 1].wait_recv()
    score_block(1, 1, 1)
    sib_got[2, 1].wait_recv()
    score_block(2, 1, 1)

    def four(c, width):
        return jnp.concatenate([lat_t[c * 4 + n, :width, :] for n in range(4)], axis=1)

    def forward():
        row_max = jnp.max(top[...], axis=0, keepdims=True)
        total = jnp.zeros((8, STACK), F32)
        for c in range(4):
            rows = slice(c * 512, (c + 1) * 512)
            e = jnp.exp2(scores[rows, :] - row_max)
            total = total + jnp.sum(e.reshape(64, 8, STACK), axis=0)
            ed[rows, STACK:] = e.astype(BF)
            add = dot(four(c, LATENT), ed[rows, STACK:])
            if c == 0:
                lift_acc[...] = add
            else:
                lift_acc[...] += add
        inverse = 1.0 / jnp.sum(total, axis=0, keepdims=True)
        lift_t[...] = (lift_acc[...] * inverse).astype(BF)
        deltas = []
        for h in range(HEADS_DEV):
            cols = slice(h * ROWS, (h + 1) * ROWS)
            o_low = dot(wv_t[cols, :], lift_t[:, cols]).astype(BF)
            o_t[cols, :] = o_low
            deltas.append(
                jnp.sum(do_t[cols, :].astype(F32) * o_low.astype(F32), axis=0, keepdims=True)
            )
            scaled = dlift[:, cols] * inverse[:, cols]
            dos_t[:, cols] = scaled.astype(BF)
            qd[STACK + h * ROWS : STACK + (h + 1) * ROWS, :] = scaled.T.astype(BF)
        delta_row[...] = jnp.concatenate(deltas, axis=1) * inverse

    forward()

    def weight_terms(n, lifted, by):
        for h in range(HEADS_DEV):
            cols = slice(h * ROWS, (h + 1) * ROWS)
            g = dot(lifted[:, cols], by[:, cols]).astype(BF)
            for piece in range(16):
                w_own[n, piece % 2, piece // 2, :, cols] = g[piece * 32 : (piece + 1) * 32, :]
        return send(w_own.at[n, 1 - core], w_sib.at[n], sib)

    def weight_sends(n, arrived):
        arrived.wait_recv()
        w_acc[n] = (w_own[n, core].astype(F32) + w_sib[n].astype(F32)).astype(BF)
        return [
            send(w_acc.at[n, x_at(i) * 2 + other(yh, dy)], w_r.at[n, m], plane[m])
            for m, (i, dy) in enumerate(plane_steps)
        ]

    def weight_end(n, arrived, ref):
        total = w_acc[n, x * 2 + yh].astype(F32)
        for m, copy in enumerate(arrived):
            copy.wait_recv()
            total = total + w_r[n, m].astype(F32)
        ref[...] = total

    def unit(i, dk):
        u = i * 2 + dk
        rows = slice(u * 256, (u + 1) * 256)
        dp = dot(lat[rows, :LATENT], dos_t[...])
        ds = (ed[rows, STACK:].astype(F32) * (dp - delta_row[...])).astype(BF)
        ed[rows, :STACK] = ds
        nope = dot(ed[rows, :], qd[...])
        rope = dot(ds, q_rope[...])
        for half in range(2):
            for dy in range(2):
                for low in range(2):
                    starts = [dy * 128 + half * 64 + n * 16 + low * 8 for n in range(4)]
                    part[u, half, dy, low, :, :LATENT] = jnp.concatenate(
                        [nope[r : r + 8, :] for r in starts], axis=0
                    ).astype(BF)
                    part[u, half, dy, low, :, LATENT:] = jnp.concatenate(
                        [rope[r : r + 8, :] for r in starts], axis=0
                    ).astype(BF)

    def to_sib(i):
        return send(part.at[i * 2 + 1], r_sib.at[i], sib)

    def on_chip(i, arrived):
        arrived.wait_recv()
        x_first[i] = (part[i * 2, 0].astype(F32) + r_sib[i, 0].astype(F32)).astype(BF)
        copy = send(x_first.at[i], r_x1.at[i - 1], along_x[i]) if i else None
        y_first[:, :, i] = (part[i * 2, 1].astype(F32) + r_sib[i, 1].astype(F32)).astype(BF)
        return copy

    def y_sends(first, count):
        which = pl.ds(first, count)
        return [
            send(y_first.at[dy, other(yl, dl), which], r_y2.at[n, which], along_y[n])
            for n, (dy, dl) in enumerate(y_steps)
        ]

    wv_sib = weight_terms(0, lift_t, do_v)
    unit(2, 1)
    sib_2 = to_sib(2)
    unit(1, 1)
    sib_1 = to_sib(1)
    wv_plane = weight_sends(0, wv_sib)
    unit(2, 0)
    x_2 = on_chip(2, sib_2)
    unit(3, 1)
    sib_3 = to_sib(3)
    unit(1, 0)
    x_1 = on_chip(1, sib_1)
    unit(0, 1)
    sib_0 = to_sib(0)
    unit(3, 0)
    x_3 = on_chip(3, sib_3)
    y_late = y_sends(1, 3)
    unit(0, 0)
    on_chip(0, sib_0)
    y_last = y_sends(0, 1)

    def query_lift_grads():
        for c in range(4):
            rows = slice(c * 512, (c + 1) * 512)
            add = dot(four(c, WIDTH), ed[rows, :STACK])
            if c == 0:
                dql[...] = add
            else:
                dql[...] += add
        lift_t[...] = (dql[:LATENT, :] * SCALE).astype(BF)

    query_lift_grads()
    wk_sib = weight_terms(1, lift_t, q_nope)

    total = x_first[0].astype(F32)
    for n, copy in enumerate([x_1, x_2, x_3]):
        copy.wait_recv()
        total = total + r_x1[n].astype(F32)
    a_1[...] = total.astype(BF)
    y_sent = [
        send(a_1.at[dy, other(yl, dl)], r_y1.at[n], along_y[n])
        for n, (dy, dl) in enumerate(y_steps)
    ]
    total = y_first[0, yl].astype(F32)
    for n in range(3):
        y_late[n].wait_recv()
        y_last[n].wait_recv()
        total = total + r_y2[n].astype(F32)
    a_2[...] = total.astype(BF)
    x_sent = [send(a_2.at[i], r_x2.at[i - 1], along_x[i]) for i in range(1, 4)]
    wk_plane = weight_sends(1, wk_sib)

    def token_outputs():
        for h in range(HEADS_DEV):
            cols = slice(h * ROWS, (h + 1) * ROWS)
            dq_t[h * QK : h * QK + NOPE, :] = dot(wk_t[cols, :], lift_t[:, cols])
            dq_t[h * QK + NOPE : (h + 1) * QK, :] = dql[LATENT:, cols] * SCALE
        dq_ref[...] = dq_t[...].T.astype(BF)
        out_ref[...] = flip(o_t[...]).astype(BF)

    token_outputs()
    weight_end(0, wv_plane, dwv_ref)

    total = a_1[0, yl].astype(F32)
    for n, copy in enumerate(y_sent):
        copy.wait_recv()
        total = total + r_y1[n].astype(F32)
    to_z[:4] = total.reshape(4, 8, WIDTH)
    total = a_2[0].astype(F32)
    for n, copy in enumerate(x_sent):
        copy.wait_recv()
        total = total + r_x2[n].astype(F32)
    to_z[4:] = total.reshape(4, 8, WIDTH)
    z_sent = [
        send(to_z.at[lax.rem(z + d, 8)], r_z.at[d - 1], along_z[d - 1]) for d in range(1, 8)
    ]
    weight_end(1, wk_plane, dwk_ref)
    total = to_z[z]
    for d, copy in enumerate(z_sent):
        copy.wait_recv()
        total = total + r_z[d]
    dlat_ref[...] = total
    for copy in started:
        copy.wait_send()


COPIES = 64


def hand_on(*refs):
    sources, targets, sem = refs[:5], refs[5:10], refs[10]
    copies = [
        pltpu.make_async_copy(src, dst, sem.at[n])
        for n, (src, dst) in enumerate(zip(sources, targets))
    ]
    for copy in copies:
        copy.start()
    for copy in copies:
        copy.wait()


def on_device(latent, query, up_key, up_value, out_grad, block_pos):
    vmem = pltpu.VMEM
    scratch = [
        vmem((SEQ, WIDTH), BF),
        vmem((16, WIDTH, ROWS), BF),
        vmem((ROWS, HEADS_DEV * QK), BF),
        vmem((LATENT, STACK), BF),
        vmem((LATENT, STACK), BF),
        vmem((ROWS, STACK), BF),
        vmem((STACK, LATENT), BF),
        vmem((STACK, LATENT), BF),
        vmem((HEADS_DEV * QK, ROWS), BF),
        vmem((STACK, ROWS), BF),
        vmem((ROWS, STACK), BF),
        vmem((WIDTH, STACK), BF),
        vmem((2 * STACK, LATENT), BF),
        vmem((STACK, ROPE), BF),
        vmem((LATENT, STACK), F32),
        vmem((LATENT, STACK), BF),
        vmem((SEQ, STACK), F32),
        vmem((SEQ, 2 * STACK), BF),
        vmem((LATENT, STACK), F32),
        vmem((LATENT, STACK), BF),
        vmem((STACK, ROWS), BF),
        vmem((HEADS_DEV * QK, ROWS), F32),
        vmem((WIDTH, STACK), F32),
        vmem((8, STACK), F32),
        vmem((1, STACK), F32),
        vmem((8, 2, 2, 2, 32, WIDTH), BF),
        vmem((4, 2, 2, 2, 32, WIDTH), BF),
        vmem((4, 2, 2, 32, WIDTH), BF),
        vmem((3, 2, 2, 32, WIDTH), BF),
        vmem((2, 2, 32, WIDTH), BF),
        vmem((3, 32, WIDTH), BF),
        vmem((2, 2, 4, 32, WIDTH), BF),
        vmem((3, 4, 32, WIDTH), BF),
        vmem((4, 32, WIDTH), BF),
        vmem((3, 32, WIDTH), BF),
        vmem((8, 8, WIDTH), F32),
        vmem((7, 8, WIDTH), F32),
        vmem((2, 2, 8, 32, STACK), BF),
        vmem((2, 8, 32, STACK), BF),
        vmem((2, 8, 32, STACK), BF),
        vmem((2, 7, 32, STACK), BF),
        pltpu.SemaphoreType.DMA((5,)),
        pltpu.SemaphoreType.DMA((COPIES,)),
        pltpu.SemaphoreType.DMA((COPIES,)),
    ]
    hbm = pl.BlockSpec(memory_space=pl.ANY)
    in_vmem = pl.BlockSpec(memory_space=pltpu.VMEM)
    shapes = (
        jax.ShapeDtypeStruct((ROWS, STACK), BF),
        jax.ShapeDtypeStruct((ROWS, HEADS_DEV * QK), BF),
        jax.ShapeDtypeStruct((8, WIDTH), F32),
        jax.ShapeDtypeStruct((32, STACK), F32),
        jax.ShapeDtypeStruct((32, STACK), F32),
    )
    results = pl.pallas_call(
        kernel,
        out_shape=shapes,
        in_specs=[hbm] * 5 + [pl.BlockSpec(memory_space=pltpu.SMEM)],
        out_specs=[in_vmem] * 5,
        scratch_shapes=scratch,
        compiler_params=pltpu.CompilerParams(
            collective_id=0, has_side_effects=True, vmem_limit_bytes=56 * 1024 * 1024
        ),
        cost_estimate=pl.CostEstimate(
            flops=7_000_000_000, bytes_accessed=4_000_000, transcendentals=1_048_576
        ),
    )(latent.T, query, up_key, up_value, out_grad, block_pos)
    return tuple(
        pl.pallas_call(
            hand_on,
            out_shape=shapes,
            in_specs=[hbm] * 5,
            out_specs=[hbm] * 5,
            scratch_shapes=[pltpu.SemaphoreType.DMA((5,))],
            compiler_params=pltpu.CompilerParams(vmem_limit_bytes=60 * 1024 * 1024),
        )(*results)
    )


def solution(mesh):
    in_specs = (
        P("ctx", None),
        P("ctx", "head"),
        P(None, "head"),
        P(None, "head"),
        P("ctx", "head"),
        P(),
    )
    out_specs = (
        P("ctx", "head"),
        P("ctx", "head"),
        P(("ctx", "head"), None),
        P("ctx", "head"),
        P("ctx", "head"),
    )
    return jax.shard_map(
        on_device, mesh=mesh, in_specs=in_specs, out_specs=out_specs, check_vma=False
    )
```

time: 521 us -> 70.5 us (0.14)
  waiting for transfers between devices: 464 us -> 0 us
  Pallas kernels: 0 us -> 68.9 us
  matrix products: 24 us -> 0 us
  between operations: 14 us -> 0.64 us
  local copies, waits for them, and re-layouts: 13.1 us -> 0 us
    unnamed x7 -> x0, waiting for transfers between devices: 407 us -> none
    pallas_call x0 -> x2, Pallas kernels: none -> 68.9 us  [the longest x1 53.3 us: on_device(): pl.pallas_call(kernel, out_shape=shapes, in_specs=[hbm] * 5 + [pl.BlockSp...]
    all_gather x1 -> x0, waiting for transfers between devices: 57 us -> none  [on_device(): key_rows, values = unpack(lax.all_gather(latent, 'ctx', axis=0, tiled=True))]
    dot_general x11 -> x0, matrix products: 24 us -> none  [the longest x1 4.5 us: update(): jnp.dot(nope_rows_t, value_low, preferred_element_type=jnp.float32)]
    unnamed x20 -> x0, local copies, waits for them, and re-layouts: 11.7 us -> none
  transfers between devices with their start and end apart: 4 -> 0, of which waited for: 4 -> 0; matrix products, arithmetic and copies ran while one was open for 5% -> 0% of each run, Pallas kernels for 0% -> 0%
where the time goes in v1:
time: 70.5 us; the launch traced here: 69.6 us
  Pallas kernels  68.9 us (98%)
    pallas_call x1, Pallas kernels, on_device(): pl.pallas_call(kernel, out_shape=shapes, in_specs=[hbm] * 5 + [pl.BlockSp...  53.3 us
    pallas_call x1, Pallas kernels, on_device(): pl.pallas_call(hand_on, out_shape=shapes, in_specs=[hbm] * 5, out_specs=[...  15.7 us

profile of v1, /device:TPU:2, one launch (start us, length us, event | category | flops | bytes accessed | tf_op | source)
XLA Modules:
  0.0 69.6 jit_solution(429024982064232614)
XLA Ops:
  0.6 53.3 %shard_map.101 = (bf16[128,512]{1,0:T(8,128)(2,1)}, bf16[128,768]{1,0:T(8,128)(2,1)}, f32[8,576]{1,0:T(8,128)}, f32[32,512]{1,0:T(8,128)}, f32[32,512]{1,0:T(8,128)}) custom-call(bf16[576,128]{1,0:T(8,128)(2,1)} %bitcast.1, bf16[128,768]{1,0:T(8,128)(2,1)} %query_hbm.1, bf16[512,512]{1,0:T(8,128)(2,1)} %wk_hbm.1, bf16[512,512]{1,0:T(8,128)(2,1)} %wv_hbm.1, ...), custom_call_target="tpu_custom_call" | custom-call | flops 7000000000 | bytes 4000000 | tf_op jit(solution)/shard_map/pallas_call | solution.py:462
  53.9 15.7 %shard_map.102 = (bf16[128,512]{1,0:T(8,128)(2,1)}, bf16[128,768]{1,0:T(8,128)(2,1)}, f32[8,576]{1,0:T(8,128)}, f32[32,512]{1,0:T(8,128)}, f32[32,512]{1,0:T(8,128)}) custom-call(bf16[128,512]{1,0:T(8,128)(2,1)} %get-tuple-element.10.refs_0_, bf16[128,768]{1,0:T(8,128)(2,1)} %get-tuple-element.11.refs_1_, f32[8,576]{1,0:T(8,128)} %get-tuple-element.12.refs_2_, ...), custom_call_target="tpu_custom_call" | custom-call | tf_op jit(solution)/shard_map/pallas_call | solution.py:476

commit v2 on v1

--- a/solution.py
+++ b/solution.py
@@ -49,7 +49,7 @@
     qs_t, qd, q_rope, dlift, dos_t, scores, ed, lift_acc, lift_t, o_t, dq_t, dql,
     top, delta_row, part, r_sib, x_first, r_x1, a_1, r_y1, y_first, r_y2, a_2, r_x2,
     to_z, r_z, w_own, w_sib, w_acc, w_r,
-    load_sem, send_sem, recv_sem,
+    out_v, dq_v, dlat_v, dwk_v, dwv_v, load_sem, store_sem, send_sem, recv_sem,
 ):
     ctx, head = lax.axis_index("ctx"), lax.axis_index("head")
     x, yh, core = lax.div(ctx, 4), lax.rem(lax.div(ctx, 2), 2), lax.rem(ctx, 2)
@@ -68,6 +68,7 @@
     y_steps = [(0, 1), (1, 0), (1, 1)]
     along_y = [dev(0, dy, 0, 0, dl) for dy, dl in y_steps]
     along_z = [dev(0, 0, 0, d, 0) for d in range(1, 8)]
+
     plane_steps = [(i, dy) for i in range(4) for dy in range(2)][1:]
     plane = [dev(i, dy, 0, 0, 0) for i, dy in plane_steps]
 
@@ -96,6 +97,7 @@
 
     def send(src, dst, to):
         n = len(started)
+        assert n < COPIES
         copy = pltpu.make_async_remote_copy(
             src_ref=src, dst_ref=dst, send_sem=send_sem.at[n], recv_sem=recv_sem.at[n],
             device_id=to, device_id_type=pl.DeviceIdType.MESH,
@@ -104,18 +106,20 @@
         started.append(copy)
         return copy
 
-    def block(i, dk, dy):
-        return lat_t.at[slot(i, dk, dy)]
+    def block(i, dk, dy, h=None):
+        if h is None:
+            return lat_t.at[slot(i, dk, dy)]
+        return lat_t.at[slot(i, dk, dy), pl.ds(h * (WIDTH // 2), WIDTH // 2)]
+
+    def send_halves(src, dst, to):
+        return [send(block(*src, h), block(*dst, h), to) for h in range(2)]
 
     def pass_on(i, dy):
         return send(block(i, 0, dy), block(i, 1, dy), sib)
 
     loads[0].wait()
-    own = lat_t.at[0]
-    from_x2 = send(own, block(2, 0, 0), along_x[2])
-    from_y = send(own, block(0, 0, 1), near_y)
-    from_x3 = send(own, block(3, 0, 0), along_x[1])
-    from_x1 = send(own, block(1, 0, 0), along_x[3])
+    from_x2 = send_halves((0, 0, 0), (2, 0, 0), along_x[2])
+    from_y = send_halves((0, 0, 0), (0, 0, 1), near_y)
     sib_got = {(0, 0): pass_on(0, 0)}
 
     for load in loads[1:]:
@@ -123,7 +127,6 @@
 
     def lift_queries():
         q_t[...] = flip(q_v[...]).astype(BF)
-        do_t[...] = flip(do_v[...]).astype(BF)
         for h in range(HEADS_DEV):
             cols = slice(h * ROWS, (h + 1) * ROWS)
             q_h_t = q_t[h * QK : h * QK + NOPE, :]
@@ -132,6 +135,8 @@
             rope_t = q_t[h * QK + NOPE : (h + 1) * QK, :].astype(F32)
             qs_t[LATENT:, cols] = (rope_t * (SCALE * LOG2E)).astype(BF)
 
+    from_x3 = send(block(0, 0, 0), block(3, 0, 0), along_x[1])
+    from_x1 = send(block(0, 0, 0), block(1, 0, 0), along_x[3])
     lift_queries()
     query_row = lax.broadcasted_iota(jnp.int32, (1, STACK), 1)
     query_pos = (
@@ -155,20 +160,23 @@
         top[...] = jnp.maximum(top[...], jnp.max(s.reshape(ROWS // 8, 8, STACK), axis=0))
 
     score_block(0, 0, 0)
-    from_y.wait_recv()
-    up_x3 = send(block(0, 0, 1), block(3, 0, 1), along_x[1])
-    up_x1 = send(block(0, 0, 1), block(1, 0, 1), along_x[3])
+    up_x3, up_x1, up_y = [], [], []
+    for h in range(2):
+        from_y[h].wait_recv()
+        up_x3.append(send(block(0, 0, 1, h), block(3, 0, 1, h), along_x[1]))
+        up_x1.append(send(block(0, 0, 1, h), block(1, 0, 1, h), along_x[3]))
     sib_got[0, 1] = pass_on(0, 1)
     sib_got[0, 0].wait_recv()
     score_block(0, 1, 0)
-    from_x2.wait_recv()
-    up_y = send(block(2, 0, 0), block(2, 0, 1), near_y)
+    for h in range(2):
+        from_x2[h].wait_recv()
+        up_y.append(send(block(2, 0, 0, h), block(2, 0, 1, h), near_y))
     sib_got[2, 0] = pass_on(2, 0)
+    score_block(0, 0, 1)
     from_x3.wait_recv()
     sib_got[3, 0] = pass_on(3, 0)
     from_x1.wait_recv()
     sib_got[1, 0] = pass_on(1, 0)
-    score_block(0, 0, 1)
     score_block(2, 0, 0)
     score_block(3, 0, 0)
     score_block(1, 0, 0)
@@ -176,6 +184,7 @@
     def lift_rest():
         wk_t[...] = flip(wk[...]).astype(BF)
         wv_t[...] = flip(wv[...]).astype(BF)
+        do_t[...] = flip(do_v[...]).astype(BF)
         for h in range(HEADS_DEV):
             cols = slice(h * ROWS, (h + 1) * ROWS)
             q_nope[:, cols] = flip(q_t[h * QK : h * QK + NOPE, :]).astype(BF)
@@ -189,15 +198,18 @@
     score_block(0, 1, 1)
     sib_got[2, 0].wait_recv()
     score_block(2, 1, 0)
-    up_x3.wait_recv()
+    for h in range(2):
+        up_x3[h].wait_recv()
     sib_got[3, 1] = pass_on(3, 1)
-    up_x1.wait_recv()
+    for h in range(2):
+        up_x1[h].wait_recv()
     sib_got[1, 1] = pass_on(1, 1)
     sib_got[3, 0].wait_recv()
     score_block(3, 1, 0)
     sib_got[1, 0].wait_recv()
     score_block(1, 1, 0)
-    up_y.wait_recv()
+    for h in range(2):
+        up_y[h].wait_recv()
     sib_got[2, 1] = pass_on(2, 1)
     score_block(3, 0, 1)
     score_block(1, 0, 1)
@@ -247,23 +259,25 @@
             cols = slice(h * ROWS, (h + 1) * ROWS)
             g = dot(lifted[:, cols], by[:, cols]).astype(BF)
             for piece in range(16):
-                w_own[n, piece % 2, piece // 2, :, cols] = g[piece * 32 : (piece + 1) * 32, :]
+                xx, yy, kk = piece // 4, piece // 2 % 2, piece % 2
+                w_own[n, kk, yy, xx, :, cols] = g[piece * 32 : (piece + 1) * 32, :]
         return send(w_own.at[n, 1 - core], w_sib.at[n], sib)
 
-    def weight_sends(n, arrived):
+    def weight_on_chip(n, arrived):
         arrived.wait_recv()
         w_acc[n] = (w_own[n, core].astype(F32) + w_sib[n].astype(F32)).astype(BF)
+
+    def weight_sends(n):
         return [
-            send(w_acc.at[n, x_at(i) * 2 + other(yh, dy)], w_r.at[n, m], plane[m])
+            send(w_acc.at[n, other(yh, dy), x_at(i)], w_r.at[n, m], plane[m])
             for m, (i, dy) in enumerate(plane_steps)
         ]
 
-    def weight_end(n, arrived, ref):
-        total = w_acc[n, x * 2 + yh].astype(F32)
-        for m, copy in enumerate(arrived):
+    def summed(total, ref, arrived):
+        for n, copy in enumerate(arrived):
             copy.wait_recv()
-            total = total + w_r[n, m].astype(F32)
-        ref[...] = total
+            total = total + ref[n].astype(F32)
+        return total
 
     def unit(i, dk):
         u = i * 2 + dk
@@ -284,6 +298,12 @@
                         [rope[r : r + 8, :] for r in starts], axis=0
                     ).astype(BF)
 
+    def y_sends(i):
+        return [
+            send(y_first.at[dy, other(yl, dl), i], r_y2.at[n, i], along_y[n])
+            for n, (dy, dl) in enumerate(y_steps)
+        ]
+
     def to_sib(i):
         return send(part.at[i * 2 + 1], r_sib.at[i], sib)
 
@@ -292,35 +312,32 @@
         x_first[i] = (part[i * 2, 0].astype(F32) + r_sib[i, 0].astype(F32)).astype(BF)
         copy = send(x_first.at[i], r_x1.at[i - 1], along_x[i]) if i else None
         y_first[:, :, i] = (part[i * 2, 1].astype(F32) + r_sib[i, 1].astype(F32)).astype(BF)
-        return copy
-
-    def y_sends(first, count):
-        which = pl.ds(first, count)
-        return [
-            send(y_first.at[dy, other(yl, dl), which], r_y2.at[n, which], along_y[n])
-            for n, (dy, dl) in enumerate(y_steps)
-        ]
-
-    wv_sib = weight_terms(0, lift_t, do_v)
+        return copy, y_sends(i)
+
+    def x_after_y(i, copies):
+        a_2[i] = summed(y_first[0, yl, i].astype(F32), r_y2.at[:, i], copies).astype(BF)
+        return send(a_2.at[i], r_x2.at[i - 1], along_x[i]) if i else None
+
     unit(2, 1)
     sib_2 = to_sib(2)
+    unit(2, 0)
+    wv_sib = weight_terms(0, lift_t, do_v)
     unit(1, 1)
     sib_1 = to_sib(1)
-    wv_plane = weight_sends(0, wv_sib)
-    unit(2, 0)
-    x_2 = on_chip(2, sib_2)
+    x_2, y_2 = on_chip(2, sib_2)
+    unit(1, 0)
     unit(3, 1)
     sib_3 = to_sib(3)
-    unit(1, 0)
-    x_1 = on_chip(1, sib_1)
+    x_1, y_1 = on_chip(1, sib_1)
+    unit(3, 0)
     unit(0, 1)
     sib_0 = to_sib(0)
-    unit(3, 0)
-    x_3 = on_chip(3, sib_3)
-    y_late = y_sends(1, 3)
+    x_3, y_3 = on_chip(3, sib_3)
     unit(0, 0)
-    on_chip(0, sib_0)
-    y_last = y_sends(0, 1)
+    _, y_0 = on_chip(0, sib_0)
+    weight_on_chip(0, wv_sib)
+    x_sent = [x_after_y(2, y_2)]
+    wv_got = weight_sends(0)
 
     def query_lift_grads():
         for c in range(4):
@@ -335,75 +352,78 @@
     query_lift_grads()
     wk_sib = weight_terms(1, lift_t, q_nope)
 
-    total = x_first[0].astype(F32)
-    for n, copy in enumerate([x_1, x_2, x_3]):
-        copy.wait_recv()
-        total = total + r_x1[n].astype(F32)
-    a_1[...] = total.astype(BF)
-    y_sent = [
-        send(a_1.at[dy, other(yl, dl)], r_y1.at[n], along_y[n])
-        for n, (dy, dl) in enumerate(y_steps)
-    ]
-    total = y_first[0, yl].astype(F32)
-    for n in range(3):
-        y_late[n].wait_recv()
-        y_last[n].wait_recv()
-        total = total + r_y2[n].astype(F32)
-    a_2[...] = total.astype(BF)
-    x_sent = [send(a_2.at[i], r_x2.at[i - 1], along_x[i]) for i in range(1, 4)]
-    wk_plane = weight_sends(1, wk_sib)
-
     def token_outputs():
         for h in range(HEADS_DEV):
             cols = slice(h * ROWS, (h + 1) * ROWS)
             dq_t[h * QK : h * QK + NOPE, :] = dot(wk_t[cols, :], lift_t[:, cols])
             dq_t[h * QK + NOPE : (h + 1) * QK, :] = dql[LATENT:, cols] * SCALE
-        dq_ref[...] = dq_t[...].T.astype(BF)
-        out_ref[...] = flip(o_t[...]).astype(BF)
+        dq_v[...] = dq_t[...].T.astype(BF)
+        out_v[...] = flip(o_t[...]).astype(BF)
 
     token_outputs()
-    weight_end(0, wv_plane, dwv_ref)
-
-    total = a_1[0, yl].astype(F32)
-    for n, copy in enumerate(y_sent):
-        copy.wait_recv()
-        total = total + r_y1[n].astype(F32)
-    to_z[:4] = total.reshape(4, 8, WIDTH)
-    total = a_2[0].astype(F32)
-    for n, copy in enumerate(x_sent):
-        copy.wait_recv()
-        total = total + r_x2[n].astype(F32)
-    to_z[4:] = total.reshape(4, 8, WIDTH)
+    stored = []
+
+    def store(src, dst):
+        copy = pltpu.make_async_copy(src, dst, store_sem.at[len(stored)])
+        copy.start()
+        stored.append(copy)
+
+    store(dq_v, dq_ref)
+    store(out_v, out_ref)
+
+    x_sent.insert(0, x_after_y(1, y_1))
+    a_1[...] = summed(x_first[0].astype(F32), r_x1, [x_1, x_2, x_3]).astype(BF)
+    y_sent = [
+        send(a_1.at[dy, other(yl, dl)], r_y1.at[n], along_y[n])
+        for n, (dy, dl) in enumerate(y_steps)
+    ]
+    x_sent.append(x_after_y(3, y_3))
+    x_after_y(0, y_0)
+    weight_on_chip(1, wk_sib)
+    wk_got = weight_sends(1)
+
+    to_z[:4] = summed(a_1[0, yl].astype(F32), r_y1, y_sent).reshape(4, 8, WIDTH)
+    to_z[4:] = summed(a_2[0].astype(F32), r_x2, x_sent).reshape(4, 8, WIDTH)
     z_sent = [
         send(to_z.at[lax.rem(z + d, 8)], r_z.at[d - 1], along_z[d - 1]) for d in range(1, 8)
     ]
-    weight_end(1, wk_plane, dwk_ref)
-    total = to_z[z]
-    for d, copy in enumerate(z_sent):
-        copy.wait_recv()
-        total = total + r_z[d]
-    dlat_ref[...] = total
+    dwv_v[...] = summed(w_acc[0, yh, x].astype(F32), w_r.at[0], wv_got)
+    store(dwv_v, dwv_ref)
+    dwk_v[...] = summed(w_acc[1, yh, x].astype(F32), w_r.at[1], wk_got)
+    store(dwk_v, dwk_ref)
+    dlat_v[...] = summed(to_z[z], r_z, z_sent)
+    store(dlat_v, dlat_ref)
+    for copy in stored:
+        copy.wait()
     for copy in started:
         copy.wait_send()
 
 
-COPIES = 64
+COPIES = 72
 
 
 def hand_on(*refs):
-    sources, targets, sem = refs[:5], refs[5:10], refs[10]
-    copies = [
-        pltpu.make_async_copy(src, dst, sem.at[n])
-        for n, (src, dst) in enumerate(zip(sources, targets))
-    ]
-    for copy in copies:
+    sources, targets, held, sem = refs[:5], refs[5:10], refs[10:15], refs[15]
+    arriving = [pltpu.make_async_copy(a, b, sem.at[0, n]) for n, (a, b) in enumerate(zip(sources, held))]
+    leaving = [pltpu.make_async_copy(a, b, sem.at[1, n]) for n, (a, b) in enumerate(zip(held, targets))]
+    for copy in arriving:
         copy.start()
-    for copy in copies:
+    for before, after in zip(arriving, leaving):
+        before.wait()
+        after.start()
+    for copy in leaving:
         copy.wait()
 
 
 def on_device(latent, query, up_key, up_value, out_grad, block_pos):
     vmem = pltpu.VMEM
+    shapes = (
+        jax.ShapeDtypeStruct((ROWS, STACK), BF),
+        jax.ShapeDtypeStruct((ROWS, HEADS_DEV * QK), BF),
+        jax.ShapeDtypeStruct((8, WIDTH), F32),
+        jax.ShapeDtypeStruct((32, STACK), F32),
+        jax.ShapeDtypeStruct((32, STACK), F32),
+    )
     scratch = [
         vmem((SEQ, WIDTH), BF),
         vmem((16, WIDTH, ROWS), BF),
@@ -442,28 +462,24 @@
         vmem((3, 32, WIDTH), BF),
         vmem((8, 8, WIDTH), F32),
         vmem((7, 8, WIDTH), F32),
-        vmem((2, 2, 8, 32, STACK), BF),
-        vmem((2, 8, 32, STACK), BF),
-        vmem((2, 8, 32, STACK), BF),
+        vmem((2, 2, 2, 4, 32, STACK), BF),
+        vmem((2, 2, 4, 32, STACK), BF),
+        vmem((2, 2, 4, 32, STACK), BF),
         vmem((2, 7, 32, STACK), BF),
+    ]
+    scratch += [vmem(shape.shape, shape.dtype) for shape in shapes]
+    scratch += [
+        pltpu.SemaphoreType.DMA((5,)),
         pltpu.SemaphoreType.DMA((5,)),
         pltpu.SemaphoreType.DMA((COPIES,)),
         pltpu.SemaphoreType.DMA((COPIES,)),
     ]
     hbm = pl.BlockSpec(memory_space=pl.ANY)
-    in_vmem = pl.BlockSpec(memory_space=pltpu.VMEM)
-    shapes = (
-        jax.ShapeDtypeStruct((ROWS, STACK), BF),
-        jax.ShapeDtypeStruct((ROWS, HEADS_DEV * QK), BF),
-        jax.ShapeDtypeStruct((8, WIDTH), F32),
-        jax.ShapeDtypeStruct((32, STACK), F32),
-        jax.ShapeDtypeStruct((32, STACK), F32),
-    )
     results = pl.pallas_call(
         kernel,
         out_shape=shapes,
         in_specs=[hbm] * 5 + [pl.BlockSpec(memory_space=pltpu.SMEM)],
-        out_specs=[in_vmem] * 5,
+        out_specs=[hbm] * 5,
         scratch_shapes=scratch,
         compiler_params=pltpu.CompilerParams(
             collective_id=0, has_side_effects=True, vmem_limit_bytes=56 * 1024 * 1024
@@ -478,7 +494,8 @@
             out_shape=shapes,
             in_specs=[hbm] * 5,
             out_specs=[hbm] * 5,
-            scratch_shapes=[pltpu.SemaphoreType.DMA((5,))],
+            scratch_shapes=[vmem(shape.shape, shape.dtype) for shape in shapes]
+            + [pltpu.SemaphoreType.DMA((2, 5))],
             compiler_params=pltpu.CompilerParams(vmem_limit_bytes=60 * 1024 * 1024),
         )(*results)
     )

time: 70.5 us -> 57.1 us (0.81)
  the two profiles are of different devices: /device:TPU:2 before, /device:TPU:24 now
where the time goes in v2:
time: 57.1 us; the launch traced here: 57 us
  Pallas kernels  56.3 us (99%)
  between operations  0.64 us (1%)
    pallas_call x1, Pallas kernels, on_device(): pl.pallas_call(kernel, out_shape=shapes, in_specs=[hbm] * 5 + [pl.BlockSp...  54.5 us
    pallas_call x1, Pallas kernels, on_device(): pl.pallas_call(hand_on, out_shape=shapes, in_specs=[hbm] * 5, out_specs=[...  1.8 us

profile of v2, /device:TPU:24, one launch (start us, length us, event | category | flops | bytes accessed | tf_op | source)
XLA Modules:
  0.0 57.0 jit_solution(4291500170382418794)
XLA Ops:
  0.6 54.5 %shard_map.101 = (bf16[128,512]{1,0:T(8,128)(2,1)}, bf16[128,768]{1,0:T(8,128)(2,1)}, f32[8,576]{1,0:T(8,128)}, f32[32,512]{1,0:T(8,128)}, f32[32,512]{1,0:T(8,128)}) custom-call(bf16[576,128]{1,0:T(8,128)(2,1)} %bitcast.1, bf16[128,768]{1,0:T(8,128)(2,1)} %query_hbm.1, bf16[512,512]{1,0:T(8,128)(2,1)} %wk_hbm.1, bf16[512,512]{1,0:T(8,128)(2,1)} %wv_hbm.1, ...), custom_call_target="tpu_custom_call" | custom-call | flops 7000000000 | bytes 4000000 | tf_op jit(solution)/shard_map/pallas_call | solution.py:478
  55.2 1.8 %shard_map.102 = (bf16[128,512]{1,0:T(8,128)(2,1)}, bf16[128,768]{1,0:T(8,128)(2,1)}, f32[8,576]{1,0:T(8,128)}, f32[32,512]{1,0:T(8,128)}, f32[32,512]{1,0:T(8,128)}) custom-call(bf16[128,512]{1,0:T(8,128)(2,1)} %get-tuple-element.10.refs_0_, bf16[128,768]{1,0:T(8,128)(2,1)} %get-tuple-element.11.refs_1_, f32[8,576]{1,0:T(8,128)} %get-tuple-element.12.refs_2_, ...), custom_call_target="tpu_custom_call" | custom-call | tf_op jit(solution)/shard_map/pallas_call | solution.py:492

commit v3 on v2

--- a/solution.py
+++ b/solution.py
@@ -18,6 +18,7 @@
 HEADS_DEV = 4
 STACK = HEADS_DEV * ROWS
 SEQ = 2048
+HALF = WIDTH // 2
 SCALE = 1.0 / math.sqrt(QK)
 LOG2E = 1.4426950408889634
 MASKED = -1e30
@@ -34,8 +35,13 @@
     return a.astype(F32).T
 
 
+EARLY = 10
+
+
 def slot(i, dk, dy):
-    return i * 4 + dk * 2 + dy
+    if i and dy:
+        return EARLY + (i - 1) * 2 + dk
+    return (dy if i == 0 else i + 1) * 2 + dk
 
 
 def other(a, flip_it):
@@ -47,9 +53,9 @@
     out_ref, dq_ref, dlat_ref, dwk_ref, dwv_ref,
     lat, lat_t, q_v, wk, wv, do_v, wk_t, wv_t, q_t, do_t, q_nope,
     qs_t, qd, q_rope, dlift, dos_t, scores, ed, lift_acc, lift_t, o_t, dq_t, dql,
-    top, delta_row, part, r_sib, x_first, r_x1, a_1, r_y1, y_first, r_y2, a_2, r_x2,
-    to_z, r_z, w_own, w_sib, w_acc, w_r,
-    out_v, dq_v, dlat_v, dwk_v, dwv_v, load_sem, store_sem, send_sem, recv_sem,
+    top, stats, rescale_row, inverse_row, delta_row, part, r_sib, x_first, r_x1, r_pair, x_half, r_half, a_1, r_y1, y_first, r_y2, a_2, r_x2,
+    to_z, r_z, w_own, w_sib, w_acc, w_x, w_col, w_y,
+    load_sem, ring_sem, send_sem, recv_sem,
 ):
     ctx, head = lax.axis_index("ctx"), lax.axis_index("head")
     x, yh, core = lax.div(ctx, 4), lax.rem(lax.div(ctx, 2), 2), lax.rem(ctx, 2)
@@ -69,8 +75,7 @@
     along_y = [dev(0, dy, 0, 0, dl) for dy, dl in y_steps]
     along_z = [dev(0, 0, 0, d, 0) for d in range(1, 8)]
 
-    plane_steps = [(i, dy) for i in range(4) for dy in range(2)][1:]
-    plane = [dev(i, dy, 0, 0, 0) for i, dy in plane_steps]
+    parity = lax.rem(z, 2)
 
     loads = [
         pltpu.make_async_copy(src, dst, load_sem.at[n])
@@ -88,10 +93,18 @@
         load.start()
 
     barrier = pltpu.get_barrier_semaphore()
-    partners = [sib] + plane + [along_y[0], along_y[2]] + along_z
+    partners = [sib] + along_x[1:] + along_y + [along_z[0], along_z[6]]
     for partner in partners:
         pl.semaphore_signal(barrier, inc=1, device_id=partner, device_id_type=pl.DeviceIdType.MESH)
     pl.semaphore_wait(barrier, len(partners))
+
+    def greet(n, d):
+        for to in (along_z[d - 1], along_z[7 - d]):
+            pl.semaphore_signal(
+                ring_sem.at[n], inc=1, device_id=to, device_id_type=pl.DeviceIdType.MESH
+            )
+
+    greet(0, 1)
 
     started = []
 
@@ -109,16 +122,24 @@
     def block(i, dk, dy, h=None):
         if h is None:
             return lat_t.at[slot(i, dk, dy)]
-        return lat_t.at[slot(i, dk, dy), pl.ds(h * (WIDTH // 2), WIDTH // 2)]
+        return lat_t.at[slot(i, dk, dy), pl.ds(pl.multiple_of(h * HALF, 16), HALF)]
 
     def send_halves(src, dst, to):
         return [send(block(*src, h), block(*dst, h), to) for h in range(2)]
 
+    def trade_quarters(*where):
+        copies = []
+        for q, to in ((0, along_z[0]), (1, along_z[6])):
+            rows = pl.ds(pl.multiple_of(parity * HALF + q * (HALF // 2), 16), HALF // 2)
+            quarter = lat_t.at[slot(*where), rows]
+            copies.append(send(quarter, quarter, to))
+        return copies
+
     def pass_on(i, dy):
         return send(block(i, 0, dy), block(i, 1, dy), sib)
 
     loads[0].wait()
-    from_x2 = send_halves((0, 0, 0), (2, 0, 0), along_x[2])
+    from_x2 = send(block(0, 0, 0, parity), block(2, 0, 0, parity), along_x[2])
     from_y = send_halves((0, 0, 0), (0, 0, 1), near_y)
     sib_got = {(0, 0): pass_on(0, 0)}
 
@@ -160,24 +181,32 @@
         top[...] = jnp.maximum(top[...], jnp.max(s.reshape(ROWS // 8, 8, STACK), axis=0))
 
     score_block(0, 0, 0)
-    up_x3, up_x1, up_y = [], [], []
-    for h in range(2):
+    pl.semaphore_wait(ring_sem.at[0], 2)
+    greet(1, 2)
+    up_x3, up_x1 = [], []
+
+    def up_x(h):
         from_y[h].wait_recv()
         up_x3.append(send(block(0, 0, 1, h), block(3, 0, 1, h), along_x[1]))
         up_x1.append(send(block(0, 0, 1, h), block(1, 0, 1, h), along_x[3]))
+
+    up_x(0)
+    from_x2.wait_recv()
+    up_y = [send(block(2, 0, 0, parity), block(2, 0, 1, parity), near_y)]
+    traded = trade_quarters(2, 0, 0)
+    up_x(1)
     sib_got[0, 1] = pass_on(0, 1)
     sib_got[0, 0].wait_recv()
     score_block(0, 1, 0)
-    for h in range(2):
-        from_x2[h].wait_recv()
-        up_y.append(send(block(2, 0, 0, h), block(2, 0, 1, h), near_y))
-    sib_got[2, 0] = pass_on(2, 0)
-    score_block(0, 0, 1)
     from_x3.wait_recv()
     sib_got[3, 0] = pass_on(3, 0)
     from_x1.wait_recv()
     sib_got[1, 0] = pass_on(1, 0)
-    score_block(2, 0, 0)
+    score_block(0, 0, 1)
+    for copy in traded:
+        copy.wait_recv()
+    up_y.append(send(block(2, 0, 0, 1 - parity), block(2, 0, 1, 1 - parity), near_y))
+    sib_got[2, 0] = pass_on(2, 0)
     score_block(3, 0, 0)
     score_block(1, 0, 0)
 
@@ -194,51 +223,55 @@
             dlift[:, cols] = dot(wv[:, cols], do_t[cols, :])
 
     lift_rest()
+    pl.semaphore_wait(ring_sem.at[1], 2)
     sib_got[0, 1].wait_recv()
     score_block(0, 1, 1)
-    sib_got[2, 0].wait_recv()
-    score_block(2, 1, 0)
-    for h in range(2):
-        up_x3[h].wait_recv()
-    sib_got[3, 1] = pass_on(3, 1)
-    for h in range(2):
-        up_x1[h].wait_recv()
-    sib_got[1, 1] = pass_on(1, 1)
+    score_block(2, 0, 0)
     sib_got[3, 0].wait_recv()
     score_block(3, 1, 0)
     sib_got[1, 0].wait_recv()
     score_block(1, 1, 0)
-    for h in range(2):
-        up_y[h].wait_recv()
-    sib_got[2, 1] = pass_on(2, 1)
-    score_block(3, 0, 1)
-    score_block(1, 0, 1)
-    score_block(2, 0, 1)
-    sib_got[3, 1].wait_recv()
-    score_block(3, 1, 1)
-    sib_got[1, 1].wait_recv()
-    score_block(1, 1, 1)
-    sib_got[2, 1].wait_recv()
-    score_block(2, 1, 1)
-
-    def four(c, width):
-        return jnp.concatenate([lat_t[c * 4 + n, :width, :] for n in range(4)], axis=1)
-
-    def forward():
-        row_max = jnp.max(top[...], axis=0, keepdims=True)
+    sib_got[2, 0].wait_recv()
+    score_block(2, 1, 0)
+
+    def side_by_side(first, count, width):
+        return jnp.concatenate(
+            [lat_t[first + n, :width, :] for n in range(count)], axis=1
+        )
+
+    def exponentials(first, last, row_max):
         total = jnp.zeros((8, STACK), F32)
-        for c in range(4):
-            rows = slice(c * 512, (c + 1) * 512)
+        for start in range(first, last, 4):
+            count = min(4, last - start)
+            rows = slice(start * ROWS, (start + count) * ROWS)
             e = jnp.exp2(scores[rows, :] - row_max)
-            total = total + jnp.sum(e.reshape(64, 8, STACK), axis=0)
+            total = total + jnp.sum(e.reshape(count * ROWS // 8, 8, STACK), axis=0)
             ed[rows, STACK:] = e.astype(BF)
-            add = dot(four(c, LATENT), ed[rows, STACK:])
-            if c == 0:
+            add = dot(side_by_side(start, count, LATENT), ed[rows, STACK:])
+            if start == 0:
                 lift_acc[...] = add
             else:
                 lift_acc[...] += add
-        inverse = 1.0 / jnp.sum(total, axis=0, keepdims=True)
+        return jnp.sum(total, axis=0, keepdims=True)
+
+    def forward_early():
+        early_max = jnp.max(top[...], axis=0, keepdims=True)
+        stats[0:1, :] = early_max
+        stats[1:2, :] = exponentials(0, EARLY, early_max)
+
+    def forward_sum():
+        early_max = stats[0:1, :]
+        row_max = jnp.max(top[...], axis=0, keepdims=True)
+        rescale = jnp.exp2(early_max - row_max)
+        rescale_row[...] = rescale
+        lift_acc[...] = lift_acc[...] * rescale
+        total = stats[1:2, :] * rescale + exponentials(EARLY, 16, row_max)
+        inverse = 1.0 / total
         lift_t[...] = (lift_acc[...] * inverse).astype(BF)
+        inverse_row[...] = inverse
+
+    def forward_rest():
+        inverse = inverse_row[...]
         deltas = []
         for h in range(HEADS_DEV):
             cols = slice(h * ROWS, (h + 1) * ROWS)
@@ -252,7 +285,25 @@
             qd[STACK + h * ROWS : STACK + (h + 1) * ROWS, :] = scaled.T.astype(BF)
         delta_row[...] = jnp.concatenate(deltas, axis=1) * inverse
 
-    forward()
+    forward_early()
+    for h in range(2):
+        up_x3[h].wait_recv()
+    sib_got[3, 1] = pass_on(3, 1)
+    for h in range(2):
+        up_x1[h].wait_recv()
+    sib_got[1, 1] = pass_on(1, 1)
+    for copy in up_y:
+        copy.wait_recv()
+    sib_got[2, 1] = pass_on(2, 1)
+    score_block(3, 0, 1)
+    score_block(1, 0, 1)
+    score_block(2, 0, 1)
+    sib_got[3, 1].wait_recv()
+    score_block(3, 1, 1)
+    sib_got[1, 1].wait_recv()
+    score_block(1, 1, 1)
+    sib_got[2, 1].wait_recv()
+    score_block(2, 1, 1)
 
     def weight_terms(n, lifted, by):
         for h in range(HEADS_DEV):
@@ -266,12 +317,17 @@
     def weight_on_chip(n, arrived):
         arrived.wait_recv()
         w_acc[n] = (w_own[n, core].astype(F32) + w_sib[n].astype(F32)).astype(BF)
-
-    def weight_sends(n):
         return [
-            send(w_acc.at[n, other(yh, dy), x_at(i)], w_r.at[n, m], plane[m])
-            for m, (i, dy) in enumerate(plane_steps)
+            send(w_acc.at[n, :, x_at(i)], w_x.at[n, i - 1], along_x[i]) for i in range(1, 4)
         ]
+
+    def weight_on_y(n, arrived):
+        w_col[n] = summed(w_acc[n, :, x].astype(F32), w_x.at[n], arrived).astype(BF)
+        return send(w_col.at[n, 1 - yh], w_y.at[n], along_y[1])
+
+    def weight_end(n, arrived):
+        arrived.wait_recv()
+        return w_col[n, yh].astype(F32) + w_y[n].astype(F32)
 
     def summed(total, ref, arrived):
         for n, copy in enumerate(arrived):
@@ -281,12 +337,21 @@
 
     def unit(i, dk):
         u = i * 2 + dk
-        rows = slice(u * 256, (u + 1) * 256)
-        dp = dot(lat[rows, :LATENT], dos_t[...])
-        ds = (ed[rows, STACK:].astype(F32) * (dp - delta_row[...])).astype(BF)
-        ed[rows, :STACK] = ds
-        nope = dot(ed[rows, :], qd[...])
-        rope = dot(ds, q_rope[...])
+        spans = [pl.ds(slot(i, dk, dy) * ROWS, ROWS) for dy in range(2)]
+
+        def both(ref, cols):
+            return jnp.concatenate([ref[rows, cols] for rows in spans], axis=0)
+
+        dp = dot(both(lat, slice(0, LATENT)), dos_t[...])
+        for dy, rows in enumerate(spans):
+            e = ed[rows, STACK:].astype(F32)
+            if slot(i, dk, dy) < EARLY:
+                e = e * rescale_row[...]
+                ed[rows, STACK:] = e.astype(BF)
+            ds = e * (dp[dy * ROWS : (dy + 1) * ROWS] - delta_row[...])
+            ed[rows, :STACK] = ds.astype(BF)
+        nope = dot(both(ed, slice(None)), qd[...])
+        rope = dot(both(ed, slice(0, STACK)), q_rope[...])
         for half in range(2):
             for dy in range(2):
                 for low in range(2):
@@ -310,7 +375,7 @@
     def on_chip(i, arrived):
         arrived.wait_recv()
         x_first[i] = (part[i * 2, 0].astype(F32) + r_sib[i, 0].astype(F32)).astype(BF)
-        copy = send(x_first.at[i], r_x1.at[i - 1], along_x[i]) if i else None
+        copy = send(x_first.at[i], r_x1.at[i // 2], along_x[i]) if i % 2 else None
         y_first[:, :, i] = (part[i * 2, 1].astype(F32) + r_sib[i, 1].astype(F32)).astype(BF)
         return copy, y_sends(i)
 
@@ -318,31 +383,41 @@
         a_2[i] = summed(y_first[0, yl, i].astype(F32), r_y2.at[:, i], copies).astype(BF)
         return send(a_2.at[i], r_x2.at[i - 1], along_x[i]) if i else None
 
+    forward_sum()
+    wv_sib = weight_terms(0, lift_t, do_v)
+    forward_rest()
     unit(2, 1)
     sib_2 = to_sib(2)
+    wv_x = weight_on_chip(0, wv_sib)
     unit(2, 0)
-    wv_sib = weight_terms(0, lift_t, do_v)
     unit(1, 1)
     sib_1 = to_sib(1)
-    x_2, y_2 = on_chip(2, sib_2)
+    _, y_2 = on_chip(2, sib_2)
+    paired = [
+        send(x_first.at[2, 1 - parity, q], r_pair.at[q], to)
+        for q, to in ((0, along_z[0]), (1, along_z[6]))
+    ]
     unit(1, 0)
     unit(3, 1)
     sib_3 = to_sib(3)
     x_1, y_1 = on_chip(1, sib_1)
+    for q, copy in enumerate(paired):
+        copy.wait_recv()
+        x_half[q] = (x_first[2, parity, q].astype(F32) + r_pair[q].astype(F32)).astype(BF)
+    x_2 = send(x_half, r_half, along_x[2])
     unit(3, 0)
     unit(0, 1)
     sib_0 = to_sib(0)
     x_3, y_3 = on_chip(3, sib_3)
     unit(0, 0)
     _, y_0 = on_chip(0, sib_0)
-    weight_on_chip(0, wv_sib)
+    wv_y = weight_on_y(0, wv_x)
     x_sent = [x_after_y(2, y_2)]
-    wv_got = weight_sends(0)
 
     def query_lift_grads():
         for c in range(4):
             rows = slice(c * 512, (c + 1) * 512)
-            add = dot(four(c, WIDTH), ed[rows, :STACK])
+            add = dot(side_by_side(c * 4, 4, WIDTH), ed[rows, :STACK])
             if c == 0:
                 dql[...] = add
             else:
@@ -357,44 +432,43 @@
             cols = slice(h * ROWS, (h + 1) * ROWS)
             dq_t[h * QK : h * QK + NOPE, :] = dot(wk_t[cols, :], lift_t[:, cols])
             dq_t[h * QK + NOPE : (h + 1) * QK, :] = dql[LATENT:, cols] * SCALE
-        dq_v[...] = dq_t[...].T.astype(BF)
-        out_v[...] = flip(o_t[...]).astype(BF)
+        dq_ref[...] = dq_t[...].T.astype(BF)
+        out_ref[...] = flip(o_t[...]).astype(BF)
 
     token_outputs()
-    stored = []
-
-    def store(src, dst):
-        copy = pltpu.make_async_copy(src, dst, store_sem.at[len(stored)])
-        copy.start()
-        stored.append(copy)
-
-    store(dq_v, dq_ref)
-    store(out_v, out_ref)
-
     x_sent.insert(0, x_after_y(1, y_1))
-    a_1[...] = summed(x_first[0].astype(F32), r_x1, [x_1, x_2, x_3]).astype(BF)
+    total = summed(x_first[0].astype(F32), r_x1, [x_1, x_3])
+    x_2.wait_recv()
+    for dy in range(2):
+        half = jnp.where(parity == dy, r_half[...].astype(F32), 0.0)
+        a_1[dy] = (total[dy] + half).astype(BF)
     y_sent = [
         send(a_1.at[dy, other(yl, dl)], r_y1.at[n], along_y[n])
         for n, (dy, dl) in enumerate(y_steps)
     ]
     x_sent.append(x_after_y(3, y_3))
     x_after_y(0, y_0)
-    weight_on_chip(1, wk_sib)
-    wk_got = weight_sends(1)
-
-    to_z[:4] = summed(a_1[0, yl].astype(F32), r_y1, y_sent).reshape(4, 8, WIDTH)
-    to_z[4:] = summed(a_2[0].astype(F32), r_x2, x_sent).reshape(4, 8, WIDTH)
+    wk_x = weight_on_chip(1, wk_sib)
+
+    def for_z(total, first):
+        for n in range(4):
+            piece = total[n * 8 : (n + 1) * 8]
+            low = jnp.concatenate([piece[:, :256], piece[:, LATENT:]], axis=1)
+            high = jnp.concatenate([piece[:, 256:LATENT], jnp.zeros((8, ROPE), F32)], axis=1)
+            to_z[first + n] = jnp.concatenate([low, high], axis=0).astype(BF)
+
+    for_z(summed(a_1[0, yl].astype(F32), r_y1, y_sent), 0)
+    for_z(summed(a_2[0].astype(F32), r_x2, x_sent), 4)
     z_sent = [
         send(to_z.at[lax.rem(z + d, 8)], r_z.at[d - 1], along_z[d - 1]) for d in range(1, 8)
     ]
-    dwv_v[...] = summed(w_acc[0, yh, x].astype(F32), w_r.at[0], wv_got)
-    store(dwv_v, dwv_ref)
-    dwk_v[...] = summed(w_acc[1, yh, x].astype(F32), w_r.at[1], wk_got)
-    store(dwk_v, dwk_ref)
-    dlat_v[...] = summed(to_z[z], r_z, z_sent)
-    store(dlat_v, dlat_ref)
-    for copy in stored:
-        copy.wait()
+    wk_y = weight_on_y(1, wk_x)
+    dwv_ref[...] = weight_end(0, wv_y)
+    total = summed(to_z[z].astype(F32), r_z, z_sent)
+    dlat_ref[:, :256] = total[:8, :256]
+    dlat_ref[:, 256:LATENT] = total[8:, :256]
+    dlat_ref[:, LATENT:] = total[:8, 256:]
+    dwk_ref[...] = weight_end(1, wk_y)
     for copy in started:
         copy.wait_send()
 
@@ -403,15 +477,14 @@
 
 
 def hand_on(*refs):
-    sources, targets, held, sem = refs[:5], refs[5:10], refs[10:15], refs[15]
-    arriving = [pltpu.make_async_copy(a, b, sem.at[0, n]) for n, (a, b) in enumerate(zip(sources, held))]
-    leaving = [pltpu.make_async_copy(a, b, sem.at[1, n]) for n, (a, b) in enumerate(zip(held, targets))]
-    for copy in arriving:
+    held, targets, sem = refs[:5], refs[5:10], refs[10]
+    copies = [
+        pltpu.make_async_copy(src, dst, sem.at[n])
+        for n, (src, dst) in enumerate(zip(held, targets))
+    ]
+    for copy in copies:
         copy.start()
-    for before, after in zip(arriving, leaving):
-        before.wait()
-        after.start()
-    for copy in leaving:
+    for copy in copies:
         copy.wait()
 
 
@@ -449,37 +522,45 @@
         vmem((HEADS_DEV * QK, ROWS), F32),
         vmem((WIDTH, STACK), F32),
         vmem((8, STACK), F32),
+        vmem((8, STACK), F32),
+        vmem((1, STACK), F32),
+        vmem((1, STACK), F32),
         vmem((1, STACK), F32),
         vmem((8, 2, 2, 2, 32, WIDTH), BF),
         vmem((4, 2, 2, 2, 32, WIDTH), BF),
         vmem((4, 2, 2, 32, WIDTH), BF),
-        vmem((3, 2, 2, 32, WIDTH), BF),
+        vmem((2, 2, 2, 32, WIDTH), BF),
+        vmem((2, 32, WIDTH), BF),
+        vmem((2, 32, WIDTH), BF),
+        vmem((2, 32, WIDTH), BF),
         vmem((2, 2, 32, WIDTH), BF),
         vmem((3, 32, WIDTH), BF),
         vmem((2, 2, 4, 32, WIDTH), BF),
         vmem((3, 4, 32, WIDTH), BF),
         vmem((4, 32, WIDTH), BF),
         vmem((3, 32, WIDTH), BF),
-        vmem((8, 8, WIDTH), F32),
-        vmem((7, 8, WIDTH), F32),
+        vmem((8, 16, 256 + ROPE), BF),
+        vmem((7, 16, 256 + ROPE), BF),
         vmem((2, 2, 2, 4, 32, STACK), BF),
         vmem((2, 2, 4, 32, STACK), BF),
         vmem((2, 2, 4, 32, STACK), BF),
-        vmem((2, 7, 32, STACK), BF),
+        vmem((2, 3, 2, 32, STACK), BF),
+        vmem((2, 2, 32, STACK), BF),
+        vmem((2, 32, STACK), BF),
     ]
-    scratch += [vmem(shape.shape, shape.dtype) for shape in shapes]
     scratch += [
         pltpu.SemaphoreType.DMA((5,)),
-        pltpu.SemaphoreType.DMA((5,)),
+        pltpu.SemaphoreType.REGULAR((2,)),
         pltpu.SemaphoreType.DMA((COPIES,)),
         pltpu.SemaphoreType.DMA((COPIES,)),
     ]
     hbm = pl.BlockSpec(memory_space=pl.ANY)
+    in_vmem = pl.BlockSpec(memory_space=pltpu.VMEM)
     results = pl.pallas_call(
         kernel,
-        out_shape=shapes,
+        out_shape=tuple(vmem(shape.shape, shape.dtype) for shape in shapes),
         in_specs=[hbm] * 5 + [pl.BlockSpec(memory_space=pltpu.SMEM)],
-        out_specs=[hbm] * 5,
+        out_specs=[in_vmem] * 5,
         scratch_shapes=scratch,
         compiler_params=pltpu.CompilerParams(
             collective_id=0, has_side_effects=True, vmem_limit_bytes=56 * 1024 * 1024
@@ -492,12 +573,10 @@
         pl.pallas_call(
             hand_on,
             out_shape=shapes,
-            in_specs=[hbm] * 5,
+            in_specs=[in_vmem] * 5,
             out_specs=[hbm] * 5,
-            scratch_shapes=[vmem(shape.shape, shape.dtype) for shape in shapes]
-            + [pltpu.SemaphoreType.DMA((2, 5))],
-            compiler_params=pltpu.CompilerParams(vmem_limit_bytes=60 * 1024 * 1024),
-        )(*results)
+            scratch_shapes=[pltpu.SemaphoreType.DMA((5,))],
+        )(*[pltpu.with_memory_space_constraint(r, pltpu.VMEM) for r in results])
     )
 
 

time: 57.1 us -> 50.2 us (0.88)
  the two profiles are of different devices: /device:TPU:24 before, /device:TPU:2 now
where the time goes in v3:
time: 50.2 us; the launch traced here: 50 us
  Pallas kernels  49.4 us (98%)
  between operations  0.64 us (1%)
    pallas_call x1, Pallas kernels, on_device(): pl.pallas_call(kernel, out_shape=tuple((vmem(shape.shape, shape.dtype) fo...  48.6 us

profile of v3, /device:TPU:2, one launch (start us, length us, event | category | flops | bytes accessed | tf_op | source)
XLA Modules:
  0.0 50.0 jit_solution(12424996299049174806)
XLA Ops:
  0.6 48.6 %shard_map.101 = (bf16[128,512]{1,0:T(8,128)(2,1)S(1)}, bf16[128,768]{1,0:T(8,128)(2,1)S(1)}, f32[8,576]{1,0:T(8,128)S(1)}, f32[32,512]{1,0:T(8,128)S(1)}, f32[32,512]{1,0:T(8,128)S(1)}) custom-call(bf16[576,128]{1,0:T(8,128)(2,1)} %bitcast.1, bf16[128,768]{1,0:T(8,128)(2,1)} %query_hbm.1, bf16[512,512]{1,0:T(8,128)(2,1)} %wk_hbm.1, ...), custom_call_target="tpu_custom_call" | custom-call | flops 7000000000 | bytes 4000000 | tf_op jit(solution)/shard_map/pallas_call | solution.py:559
  49.2 0.8 %shard_map.102 = (bf16[128,512]{1,0:T(8,128)(2,1)}, bf16[128,768]{1,0:T(8,128)(2,1)}, f32[8,576]{1,0:T(8,128)}, f32[32,512]{1,0:T(8,128)}, f32[32,512]{1,0:T(8,128)}) custom-call(bf16[128,512]{1,0:T(8,128)(2,1)S(1)} %get-tuple-element.10.refs_0_, bf16[128,768]{1,0:T(8,128)(2,1)S(1)} %get-tuple-element.11.refs_1_, f32[8,576]{1,0:T(8,128)S(1)} %get-tuple-element.12.refs_2_, ...), custom_call_target="tpu_custom_call" | custom-call | tf_op jit(solution)/shard_map/pallas_call | solution.py:573

commit v4 on v3

--- a/solution.py
+++ b/solution.py
@@ -54,7 +54,7 @@
     lat, lat_t, q_v, wk, wv, do_v, wk_t, wv_t, q_t, do_t, q_nope,
     qs_t, qd, q_rope, dlift, dos_t, scores, ed, lift_acc, lift_t, o_t, dq_t, dql,
     top, stats, rescale_row, inverse_row, delta_row, part, r_sib, x_first, r_x1, r_pair, x_half, r_half, a_1, r_y1, y_first, r_y2, a_2, r_x2,
-    to_z, r_z, w_own, w_sib, w_acc, w_x, w_col, w_y,
+    to_z, r_z, w_own, w_sib, w_acc, w_x, w_col, w_y, w_r,
     load_sem, ring_sem, send_sem, recv_sem,
 ):
     ctx, head = lax.axis_index("ctx"), lax.axis_index("head")
@@ -76,6 +76,8 @@
     along_z = [dev(0, 0, 0, d, 0) for d in range(1, 8)]
 
     parity = lax.rem(z, 2)
+    plane_steps = [(i, dy) for i in range(4) for dy in range(2)][1:]
+    plane = [dev(i, dy, 0, 0, 0) for i, dy in plane_steps]
 
     loads = [
         pltpu.make_async_copy(src, dst, load_sem.at[n])
@@ -135,13 +137,20 @@
             copies.append(send(quarter, quarter, to))
         return copies
 
-    def pass_on(i, dy):
-        return send(block(i, 0, dy), block(i, 1, dy), sib)
+    sib_got = {}
+
+    def pass_on(i, dy, h=None):
+        copy = send(block(i, 0, dy, h), block(i, 1, dy, h), sib)
+        sib_got.setdefault((i, dy), []).append(copy)
+
+    def passed(i, dy):
+        for copy in sib_got[i, dy]:
+            copy.wait_recv()
 
     loads[0].wait()
     from_x2 = send(block(0, 0, 0, parity), block(2, 0, 0, parity), along_x[2])
     from_y = send_halves((0, 0, 0), (0, 0, 1), near_y)
-    sib_got = {(0, 0): pass_on(0, 0)}
+    pass_on(0, 0)
 
     for load in loads[1:]:
         load.wait()
@@ -195,18 +204,18 @@
     up_y = [send(block(2, 0, 0, parity), block(2, 0, 1, parity), near_y)]
     traded = trade_quarters(2, 0, 0)
     up_x(1)
-    sib_got[0, 1] = pass_on(0, 1)
-    sib_got[0, 0].wait_recv()
+    pass_on(0, 1)
+    passed(0, 0)
     score_block(0, 1, 0)
     from_x3.wait_recv()
-    sib_got[3, 0] = pass_on(3, 0)
+    pass_on(3, 0)
     from_x1.wait_recv()
-    sib_got[1, 0] = pass_on(1, 0)
+    pass_on(1, 0)
     score_block(0, 0, 1)
     for copy in traded:
         copy.wait_recv()
     up_y.append(send(block(2, 0, 0, 1 - parity), block(2, 0, 1, 1 - parity), near_y))
-    sib_got[2, 0] = pass_on(2, 0)
+    pass_on(2, 0)
     score_block(3, 0, 0)
     score_block(1, 0, 0)
 
@@ -224,14 +233,14 @@
 
     lift_rest()
     pl.semaphore_wait(ring_sem.at[1], 2)
-    sib_got[0, 1].wait_recv()
+    passed(0, 1)
     score_block(0, 1, 1)
     score_block(2, 0, 0)
-    sib_got[3, 0].wait_recv()
+    passed(3, 0)
     score_block(3, 1, 0)
-    sib_got[1, 0].wait_recv()
+    passed(1, 0)
     score_block(1, 1, 0)
-    sib_got[2, 0].wait_recv()
+    passed(2, 0)
     score_block(2, 1, 0)
 
     def side_by_side(first, count, width):
@@ -286,23 +295,21 @@
         delta_row[...] = jnp.concatenate(deltas, axis=1) * inverse
 
     forward_early()
-    for h in range(2):
+    for h, y_half in ((0, parity), (1, 1 - parity)):
         up_x3[h].wait_recv()
-    sib_got[3, 1] = pass_on(3, 1)
-    for h in range(2):
+        pass_on(3, 1, h)
         up_x1[h].wait_recv()
-    sib_got[1, 1] = pass_on(1, 1)
-    for copy in up_y:
-        copy.wait_recv()
-    sib_got[2, 1] = pass_on(2, 1)
+        pass_on(1, 1, h)
+        up_y[h].wait_recv()
+        pass_on(2, 1, y_half)
     score_block(3, 0, 1)
     score_block(1, 0, 1)
     score_block(2, 0, 1)
-    sib_got[3, 1].wait_recv()
+    passed(3, 1)
     score_block(3, 1, 1)
-    sib_got[1, 1].wait_recv()
+    passed(1, 1)
     score_block(1, 1, 1)
-    sib_got[2, 1].wait_recv()
+    passed(2, 1)
     score_block(2, 1, 1)
 
     def weight_terms(n, lifted, by):
@@ -317,17 +324,19 @@
     def weight_on_chip(n, arrived):
         arrived.wait_recv()
         w_acc[n] = (w_own[n, core].astype(F32) + w_sib[n].astype(F32)).astype(BF)
+
+    def weight_on_x(n):
+        return [send(w_acc.at[n, :, x_at(i)], w_x.at[i - 1], along_x[i]) for i in range(1, 4)]
+
+    def weight_on_y(n, arrived):
+        w_col[...] = summed(w_acc[n, :, x].astype(F32), w_x, arrived).astype(BF)
+        return send(w_col.at[1 - yh], w_y, along_y[1])
+
+    def weight_direct(n):
         return [
-            send(w_acc.at[n, :, x_at(i)], w_x.at[n, i - 1], along_x[i]) for i in range(1, 4)
+            send(w_acc.at[n, other(yh, dy), x_at(i)], w_r.at[m], plane[m])
+            for m, (i, dy) in enumerate(plane_steps)
         ]
-
-    def weight_on_y(n, arrived):
-        w_col[n] = summed(w_acc[n, :, x].astype(F32), w_x.at[n], arrived).astype(BF)
-        return send(w_col.at[n, 1 - yh], w_y.at[n], along_y[1])
-
-    def weight_end(n, arrived):
-        arrived.wait_recv()
-        return w_col[n, yh].astype(F32) + w_y[n].astype(F32)
 
     def summed(total, ref, arrived):
         for n, copy in enumerate(arrived):
@@ -388,7 +397,8 @@
     forward_rest()
     unit(2, 1)
     sib_2 = to_sib(2)
-    wv_x = weight_on_chip(0, wv_sib)
+    weight_on_chip(0, wv_sib)
+    wv_x = weight_on_x(0)
     unit(2, 0)
     unit(1, 1)
     sib_1 = to_sib(1)
@@ -448,7 +458,8 @@
     ]
     x_sent.append(x_after_y(3, y_3))
     x_after_y(0, y_0)
-    wk_x = weight_on_chip(1, wk_sib)
+    weight_on_chip(1, wk_sib)
+    wk_got = weight_direct(1)
 
     def for_z(total, first):
         for n in range(4):
@@ -462,18 +473,18 @@
     z_sent = [
         send(to_z.at[lax.rem(z + d, 8)], r_z.at[d - 1], along_z[d - 1]) for d in range(1, 8)
     ]
-    wk_y = weight_on_y(1, wk_x)
-    dwv_ref[...] = weight_end(0, wv_y)
+    wv_y.wait_recv()
+    dwv_ref[...] = w_col[yh].astype(F32) + w_y[...].astype(F32)
     total = summed(to_z[z].astype(F32), r_z, z_sent)
     dlat_ref[:, :256] = total[:8, :256]
     dlat_ref[:, 256:LATENT] = total[8:, :256]
     dlat_ref[:, LATENT:] = total[:8, 256:]
-    dwk_ref[...] = weight_end(1, wk_y)
+    dwk_ref[...] = summed(w_acc[1, yh, x].astype(F32), w_r, wk_got)
     for copy in started:
         copy.wait_send()
 
 
-COPIES = 72
+COPIES = 80
 
 
 def hand_on(*refs):
@@ -544,9 +555,10 @@
         vmem((2, 2, 2, 4, 32, STACK), BF),
         vmem((2, 2, 4, 32, STACK), BF),
         vmem((2, 2, 4, 32, STACK), BF),
-        vmem((2, 3, 2, 32, STACK), BF),
-        vmem((2, 2, 32, STACK), BF),
+        vmem((3, 2, 32, STACK), BF),
         vmem((2, 32, STACK), BF),
+        vmem((32, STACK), BF),
+        vmem((7, 32, STACK), BF),
     ]
     scratch += [
         pltpu.SemaphoreType.DMA((5,)),

time: 50.2 us -> 52.1 us (1.038)
  Pallas kernels: 49.4 us -> 51.4 us
    pallas_call x1, Pallas kernels: 48.6 us -> 50.5 us  [on_device(): pl.pallas_call(kernel, out_shape=tuple((vmem(shape.shape, shape.dtype) fo...]
where the time goes in v4:
time: 52.1 us; the launch traced here: 52 us
  Pallas kernels  51.4 us (99%)
  between operations  0.64 us (1%)
    pallas_call x1, Pallas kernels, on_device(): pl.pallas_call(kernel, out_shape=tuple((vmem(shape.shape, shape.dtype) fo...  50.5 us

profile of v4, /device:TPU:2, one launch (start us, length us, event | category | flops | bytes accessed | tf_op | source)
XLA Modules:
  0.0 52.0 jit_solution(3358608335723580811)
XLA Ops:
  0.6 50.5 %shard_map.101 = (bf16[128,512]{1,0:T(8,128)(2,1)S(1)}, bf16[128,768]{1,0:T(8,128)(2,1)S(1)}, f32[8,576]{1,0:T(8,128)S(1)}, f32[32,512]{1,0:T(8,128)S(1)}, f32[32,512]{1,0:T(8,128)S(1)}) custom-call(bf16[576,128]{1,0:T(8,128)(2,1)} %bitcast.1, bf16[128,768]{1,0:T(8,128)(2,1)} %query_hbm.1, bf16[512,512]{1,0:T(8,128)(2,1)} %wk_hbm.1, ...), custom_call_target="tpu_custom_call" | custom-call | flops 7000000000 | bytes 4000000 | tf_op jit(solution)/shard_map/pallas_call | solution.py:571
  51.2 0.8 %shard_map.102 = (bf16[128,512]{1,0:T(8,128)(2,1)}, bf16[128,768]{1,0:T(8,128)(2,1)}, f32[8,576]{1,0:T(8,128)}, f32[32,512]{1,0:T(8,128)}, f32[32,512]{1,0:T(8,128)}) custom-call(bf16[128,512]{1,0:T(8,128)(2,1)S(1)} %get-tuple-element.10.refs_0_, bf16[128,768]{1,0:T(8,128)(2,1)S(1)} %get-tuple-element.11.refs_1_, f32[8,576]{1,0:T(8,128)S(1)} %get-tuple-element.12.refs_2_, ...), custom_call_target="tpu_custom_call" | custom-call | tf_op jit(solution)/shard_map/pallas_call | solution.py:585
